TPU v7x, 32 devices: a whole 2x2x4 slice. The times are simulated.
32 devices in a mesh: dp: 4 (over y, core), fsdp: 8 (over z, x).
Axes of the slice: x: 2, y: 2, z: 4, core: 2. Of those that a mesh axis runs over, the one named last changes fastest.
Arguments:
- grad_q: bfloat16 [4, 8192, 8192], P('dp', 'fsdp'), may hold values from -40 to 40, as said below
- grad_k: bfloat16 [4, 8192, 1024], P('dp', 'fsdp'), may hold values from -40 to 40
- grad_v: bfloat16 [4, 8192, 1024], P('dp', 'fsdp'), may hold values from -40 to 40
- proj_q: bfloat16 [8192, 512], P('fsdp'), may hold values from -5 to 5, as said below
- proj_k: bfloat16 [8192, 512], P('fsdp'), may hold values from -5 to 5
- proj_v: bfloat16 [8192, 512], P('fsdp'), may hold values from -5 to 5
- weight_q: bfloat16 [8192, 8192], P('fsdp', 'dp'), may hold values from -4 to 4
- key_weight_matrix: bfloat16 [8192, 1024], P('fsdp', 'dp'), may hold values from -4 to 4
- value_weight_matrix: bfloat16 [8192, 1024], P('fsdp', 'dp'), may hold values from -4 to 4
- comp_q: bfloat16 [8192, 8192], P('fsdp', 'dp'), may hold values from -0.0039978027 to 0.0039978027
- key_compensation: bfloat16 [8192, 1024], P('fsdp', 'dp'), may hold values from -0.0039978027 to 0.0039978027
- value_compensation: bfloat16 [8192, 1024], P('fsdp', 'dp'), may hold values from -0.0039978027 to 0.0039978027
- avg_q: float32 [512, 8192], P('fsdp', 'dp'), may hold values from -1.5 to 1.5
- key_first_moment: float32 [512, 1024], P('fsdp', 'dp'), may hold values from -1.5 to 1.5
- value_first_moment: float32 [512, 1024], P('fsdp', 'dp'), may hold values from -1.5 to 1.5
- sq_q: float32 [512, 8192], P('fsdp', 'dp'), may hold values from 0.001 to 0.1
- key_second_moment: float32 [512, 1024], P('fsdp', 'dp'), may hold values from 0.001 to 0.1
- value_second_moment: float32 [512, 1024], P('fsdp', 'dp'), may hold values from 0.001 to 0.1
Outputs:
- new_weight_q: float32 [8192, 8192], P('fsdp', 'dp')
- new_weight_k: float32 [8192, 1024], P('fsdp', 'dp')
- new_weight_v: float32 [8192, 1024], P('fsdp', 'dp')
- new_avg_q: float32 [512, 8192], P('fsdp', 'dp')
- new_avg_k: float32 [512, 1024], P('fsdp', 'dp')
- new_avg_v: float32 [512, 1024], P('fsdp', 'dp')
- new_sq_q: float32 [512, 8192], P('fsdp', 'dp')
- new_sq_k: float32 [512, 1024], P('fsdp', 'dp')
- new_sq_v: float32 [512, 1024], P('fsdp', 'dp')
Inputs may be any that keep to these rules, and one draw needn't show every extreme that they name: `grad_q`: each partial of the gradients is real-valued and of full rank. `proj_q`: projectors are real-valued and of full rank 512.
All inputs are finite; a program needn't handle non-finite values.
Results may differ from a plain program's by a relative error of at most 0.00044.
Values may be sent and summed in bfloat16 or wider, within the bound.
A program may use at most 128 MiB of HBM per device.

v0:
```python
import math

import jax
import jax.numpy as jnp
from jax import lax
from jax.sharding import PartitionSpec as P

QUERY_OUTPUTS = 8192
KEY_VALUE_OUTS = 1024
PROJECT_RANK = 512
STEP = 10


def adam_apply(projected, clip_factor, first_moment, second_moment):
    scaled = clip_factor * projected
    new_avg = 0.9 * first_moment + 0.1 * scaled
    new_sq = 0.95 * second_moment + 0.05 * scaled * scaled
    correct_one = 1.0 - 0.9**STEP
    correct_two = 1.0 - 0.95**STEP
    update = new_avg / correct_one / (jnp.sqrt(new_sq / correct_two) + 1e-08)
    return (new_avg, new_sq, update.astype(jnp.bfloat16))


def shards(
    grad_q,
    grad_k,
    grad_v,
    proj_q,
    proj_k,
    proj_v,
    weight_q,
    key_weight_matrix,
    value_weight_matrix,
    comp_q,
    key_compensation,
    value_compensation,
    avg_q,
    key_first_moment,
    value_first_moment,
    sq_q,
    key_second_moment,
    value_second_moment,
):
    gradients = (grad_q[0], grad_k[0], grad_v[0])
    projectors = (proj_q, proj_k, proj_v)
    weights = (weight_q, key_weight_matrix, value_weight_matrix)
    comps = (comp_q, key_compensation, value_compensation)
    avgs = (avg_q, key_first_moment, value_first_moment)
    squares = (sq_q, key_second_moment, value_second_moment)
    contract_rows = (((0,), (0,)), ((), ()))
    complete = [
        lax.dot_general(projector, gradient, contract_rows, preferred_element_type=jnp.float32)
        for gradient, projector in zip(gradients, projectors)
    ]
    narrow = (
        lax.psum_scatter(complete[0], "dp", scatter_dimension=1, tiled=True),
        lax.psum_scatter(complete[1], "dp", scatter_dimension=1, tiled=True),
        lax.psum_scatter(complete[2], "dp", scatter_dimension=1, tiled=True),
    )
    shares = (
        lax.psum_scatter(narrow[0], "fsdp", scatter_dimension=0, tiled=True),
        lax.psum_scatter(narrow[1], "fsdp", scatter_dimension=0, tiled=True),
        lax.psum_scatter(narrow[2], "fsdp", scatter_dimension=0, tiled=True),
    )
    local_sum = jnp.zeros((), jnp.float32)
    for member in shares:
        local_sum = local_sum + jnp.sum(member * member)
    square_sum = lax.psum(local_sum, ("dp", "fsdp"))
    clipping_threshold = math.sqrt(PROJECT_RANK * (QUERY_OUTPUTS + 2 * KEY_VALUE_OUTS))
    clip_factor = jnp.minimum(1.0, clipping_threshold / jnp.sqrt(square_sum + 1e-06))
    new_avgs, new_sqs, updates = ([], [], [])
    for index_mat in range(3):
        new_avg, new_sq, update = adam_apply(
            shares[index_mat], clip_factor, avgs[index_mat], squares[index_mat]
        )
        new_avgs.append(new_avg)
        new_sqs.append(new_sq)
        updates.append(update)
    zero_sums = tuple((jnp.zeros(weight.shape, jnp.float32) for weight in weights))
    pieces = (
        lax.all_gather(updates[0], "fsdp", axis=0, tiled=True),
        lax.all_gather(updates[1], "fsdp", axis=0, tiled=True),
        lax.all_gather(updates[2], "fsdp", axis=0, tiled=True),
    )
    results = []
    for total_acc, piece, projector in zip(zero_sums, pieces, projectors):
        results.append(jnp.dot(projector, piece, preferred_element_type=jnp.float32))
    products = (results[0], results[1], results[2])
    new_weights = []
    for index_mat in range(3):
        delta = -0.04 * products[index_mat]
        new_weights.append(
            weights[index_mat].astype(jnp.float32) + (delta + comps[index_mat].astype(jnp.float32))
        )
    return (
        new_weights[0],
        new_weights[1],
        new_weights[2],
        new_avgs[0],
        new_avgs[1],
        new_avgs[2],
        new_sqs[0],
        new_sqs[1],
        new_sqs[2],
    )


def solution(mesh):
    in_specs = (
        P("dp", "fsdp", None),
        P("dp", "fsdp", None),
        P("dp", "fsdp", None),
        P("fsdp", None),
        P("fsdp", None),
        P("fsdp", None),
        P("fsdp", "dp"),
        P("fsdp", "dp"),
        P("fsdp", "dp"),
        P("fsdp", "dp"),
        P("fsdp", "dp"),
        P("fsdp", "dp"),
        P("fsdp", "dp"),
        P("fsdp", "dp"),
        P("fsdp", "dp"),
        P("fsdp", "dp"),
        P("fsdp", "dp"),
        P("fsdp", "dp"),
    )
    out_specs = (
        P("fsdp", "dp"),
        P("fsdp", "dp"),
        P("fsdp", "dp"),
        P("fsdp", "dp"),
        P("fsdp", "dp"),
        P("fsdp", "dp"),
        P("fsdp", "dp"),
        P("fsdp", "dp"),
        P("fsdp", "dp"),
    )
    return jax.shard_map(shards, mesh=mesh, in_specs=in_specs, out_specs=out_specs, check_vma=False)
```

profile of v0, /device:TPU:0, one launch (start us, length us, event | category | flops | bytes accessed | tf_op | source)
XLA Modules:
  0.0 597.3 jit_solution(3964292763301466934)
XLA Ops:
  8.8 3.8 fusion.5
  12.7 4.3 fusion.3
  17.0 15.8 %fusion = f32[512,8192]{1,0:T(8,128)} fusion(bf16[1024,512]{1,0:T(8,128)(2,1)S(1)} %copy-done.2, bf16[1,1024,8192]{2,1,0:T(8,128)(2,1)} %param.18), kind=kOutput, calls=%fused_computation | convolution fusion | flops 8589934592 | bytes 34603008 | tf_op jit(solution)/shard_map/dot_general | solution.py:52
  32.9 14.0 %reduce-scatter.11.cloned.1.call-done = f32[512,256]{1,0:T(8,128)} async-done(((f32[512,1024]{1,0:T(8,128)}), f32[512,256]{1,0:T(8,128)}) %reduce-scatter.11.cloned.1.call-update) | async-done | bytes 524304 | tf_op jit(solution)/shard_map/reduce_scatter | solution.py:57
  47.0 34.1 %reduce-scatter.15.cloned.1.call-done = f32[512,256]{1,0:T(8,128)} async-done(((f32[512,1024]{1,0:T(8,128)}), f32[512,256]{1,0:T(8,128)}) %reduce-scatter.15.cloned.1.call-update) | async-done | bytes 524304 | tf_op jit(solution)/shard_map/reduce_scatter | solution.py:58
  81.1 128.7 %reduce-scatter.7.cloned.1.call-done = f32[512,2048]{1,0:T(8,128)} async-done(((f32[512,8192]{1,0:T(8,128)}), f32[512,2048]{1,0:T(8,128)}) %reduce-scatter.7.cloned.1.call-update) | async-done | bytes 4194320 | tf_op jit(solution)/shard_map/reduce_scatter | solution.py:56
  209.9 65.3 %reduce-scatter.13.cloned.1.call-done = f32[64,256]{1,0:T(8,128)} async-done(((f32[512,256]{1,0:T(8,128)}), f32[64,256]{1,0:T(8,128)}) %reduce-scatter.13.cloned.1.call-update) | async-done | bytes 65552 | tf_op jit(solution)/shard_map/reduce_scatter | solution.py:62
  276.7 62.8 %reduce-scatter.17.cloned.1.call-done = f32[64,256]{1,0:T(8,128)} async-done(((f32[512,256]{1,0:T(8,128)}), f32[64,256]{1,0:T(8,128)}) %reduce-scatter.17.cloned.1.call-update) | async-done | bytes 65552 | tf_op jit(solution)/shard_map/reduce_scatter | solution.py:63
  340.9 89.4 %reduce-scatter.9.cloned.1.call-done = f32[64,2048]{1,0:T(8,128)} async-done(((f32[512,2048]{1,0:T(8,128)}), f32[64,2048]{1,0:T(8,128)}) %reduce-scatter.9.cloned.1.call-update) | async-done | bytes 524304 | tf_op jit(solution)/shard_map/reduce_scatter | solution.py:61
  430.3 1.8 multiply_reduce_fusion
  434.0 40.3 %psum.7 = f32[]{:T(128)} all-reduce(f32[]{:T(128)S(6)} %add.72), channel_id=1, replica_groups=mesh['dp'=4,'fsdp'=8] {'dp','fsdp'}, use_global_device_ids=true, to_apply=%region_9.0 | all-reduce | flops 1 | bytes 8 | tf_op jit(solution)/shard_map/psum | solution.py:68
  475.1 2.3 divide_convert_fusion
  477.4 6.4 %copy.27 = bf16[1024,2048]{0,1:T(8,128)(2,1)} copy(bf16[1024,2048]{1,0:T(8,128)(2,1)} %param.24) | data formatting | bytes 8388608 | tf_op args[6]
  483.8 6.4 %copy.28 = bf16[1024,2048]{0,1:T(8,128)(2,1)} copy(bf16[1024,2048]{1,0:T(8,128)(2,1)} %param.27) | data formatting | bytes 8388608 | tf_op args[9]
  490.3 2.2 copy.29
  492.4 2.0 copy.30
  494.5 2.1 copy.31
  496.6 2.0 copy.32
  499.3 31.6 %all_gather.10 = bf16[512,256]{1,0:T(8,128)(2,1)S(1)} all-gather(bf16[64,256]{1,0:T(8,128)(2,1)S(1)} %get-tuple-element.21), channel_id=1, replica_groups=mesh['dp'=4,'fsdp'=8] {'fsdp'}, dimensions={0}, use_global_device_ids=true | all-gather | bytes 294912 | tf_op jit(solution)/shard_map/all_gather | solution.py:82
  530.9 2.7 fusion.12
  533.6 2.5 copy.34
  536.8 30.9 %all_gather.11 = bf16[512,256]{1,0:T(8,128)(2,1)S(1)} all-gather(bf16[64,256]{1,0:T(8,128)(2,1)S(1)} %get-tuple-element.18), channel_id=1, replica_groups=mesh['dp'=4,'fsdp'=8] {'fsdp'}, dimensions={0}, use_global_device_ids=true | all-gather | bytes 294912 | tf_op jit(solution)/shard_map/all_gather | solution.py:83
  570.8 10.4 %fusion.2 = f32[1024,2048]{0,1:T(8,128)} fusion(bf16[1024,2048]{0,1:T(8,128)(2,1)} %copy.28, bf16[1024,2048]{0,1:T(8,128)(2,1)} %copy.27, bf16[512,2048]{1,0:T(8,128)(2,1)} %all-gather.2.cloned.1.call-done, bf16[1024,512]{1,0:T(8,128)(2,1)S(1)} %copy-done.2), kind=kOutput, calls=%fused_computation.3 | convolution fusion | flops 2157969408 | bytes 19922944 | tf_op jit(solution)/shard_map/dot_general | solution.py:87
  581.1 9.3 %copy.33 = f32[1024,2048]{1,0:T(8,128)} copy(f32[1024,2048]{0,1:T(8,128)} %fusion.2) | data formatting | bytes 16777216
  (47 shorter events, 9.3 us)
Async XLA Ops:
  7.2 1.6 copy-start
  7.2 5.5 copy-start.4
  7.2 39.7 %reduce-scatter.11.cloned.1.call-start = ((), (), s32[]{:S(2)}) async-start(), calls=%async_computation.8 | async-start | bytes 2621440 | tf_op jit(solution)/shard_map/reduce_scatter | solution.py:57
  12.6 4.4 copy-start.2
  12.6 68.4 %reduce-scatter.15.cloned.1.call-start = ((), (), s32[]{:S(2)}) async-start(), calls=%async_computation.10 | async-start | bytes 2621440 | tf_op jit(solution)/shard_map/reduce_scatter | solution.py:58
  17.0 192.9 %reduce-scatter.7.cloned.1.call-start = ((), (), s32[]{:S(2)}) async-start(), calls=%async_computation.6 | async-start | bytes 20971520 | tf_op jit(solution)/shard_map/reduce_scatter | solution.py:56
  32.8 442.2 %copy-start.5 = (f32[64,2048]{1,0:T(8,128)S(1)}, f32[64,2048]{1,0:T(8,128)}, u32[]{:S(2)}) copy-start(f32[64,2048]{1,0:T(8,128)} %param.30) | copy-start | bytes 1572868
  32.9 442.2 %copy-start.6 = (f32[64,2048]{1,0:T(8,128)S(1)}, f32[64,2048]{1,0:T(8,128)}, u32[]{:S(2)}) copy-start(f32[64,2048]{1,0:T(8,128)} %param.33) | copy-start | bytes 1572868
  32.9 242.3 %reduce-scatter.13.cloned.1.call-start = ((), (), s32[]{:S(2)}) async-start(), calls=%async_computation.9 | async-start | bytes 589824 | tf_op jit(solution)/shard_map/reduce_scatter | solution.py:62
  46.9 292.5 %reduce-scatter.17.cloned.1.call-start = ((), (), s32[]{:S(2)}) async-start(), calls=%async_computation.11 | async-start | bytes 589824 | tf_op jit(solution)/shard_map/reduce_scatter | solution.py:63
  81.1 349.2 %reduce-scatter.9.cloned.1.call-start = ((), (), s32[]{:S(2)}) async-start(), calls=%async_computation.7 | async-start | bytes 4718592 | tf_op jit(solution)/shard_map/reduce_scatter | solution.py:61
  209.9 360.9 %all-gather.2.cloned.1.call-start = ((), (), s32[]{:S(2)}) async-start(), calls=%async_computation.12 | async-start | bytes 2359296 | tf_op jit(solution)/shard_map/all_gather | solution.py:81
  490.3 8.3 %copy-start.7 = (f32[64,256]{1,0:T(8,128)S(1)}, f32[64,256]{1,0:T(8,128)}, u32[]{:S(2)}) copy-start(f32[64,256]{1,0:T(8,128)} %reduce-scatter.13.cloned.1.call-done) | copy-start | bytes 196612
  490.3 8.3 %copy-start.9 = (f32[64,256]{1,0:T(8,128)S(1)}, f32[64,256]{1,0:T(8,128)}, u32[]{:S(2)}) copy-start(f32[64,256]{1,0:T(8,128)} %param.31) | copy-start | bytes 196612
  490.3 8.3 %copy-start.10 = (f32[64,256]{1,0:T(8,128)S(1)}, f32[64,256]{1,0:T(8,128)}, u32[]{:S(2)}) copy-start(f32[64,256]{1,0:T(8,128)} %param.34) | copy-start | bytes 196612
  490.3 40.6 %copy-start.3 = (bf16[1024,512]{1,0:T(8,128)(2,1)S(1)}, bf16[1024,512]{1,0:T(8,128)(2,1)}, u32[]{:S(2)}) copy-start(bf16[1024,512]{1,0:T(8,128)(2,1)} %param.22) | copy-start | bytes 3145732
  494.5 41.7 %copy-start.8 = (f32[64,256]{1,0:T(8,128)S(1)}, f32[64,256]{1,0:T(8,128)}, u32[]{:S(2)}) copy-start(f32[64,256]{1,0:T(8,128)} %reduce-scatter.17.cloned.1.call-done) | copy-start | bytes 196612
  494.5 41.7 %copy-start.11 = (f32[64,256]{1,0:T(8,128)S(1)}, f32[64,256]{1,0:T(8,128)}, u32[]{:S(2)}) copy-start(f32[64,256]{1,0:T(8,128)} %param.32) | copy-start | bytes 196612
  494.5 41.7 %copy-start.12 = (f32[64,256]{1,0:T(8,128)S(1)}, f32[64,256]{1,0:T(8,128)}, u32[]{:S(2)}) copy-start(f32[64,256]{1,0:T(8,128)} %param.35) | copy-start | bytes 196612
  581.1 9.3 %copy-start.1 = (bf16[1,1024,1024]{2,1,0:T(8,128)(2,1)S(1)}, bf16[1,1024,1024]{2,1,0:T(8,128)(2,1)}, u32[]{:S(2)}) copy-start(bf16[1,1024,1024]{2,1,0:T(8,128)(2,1)} %param.19) | copy-start | bytes 6291460
Sparse Core Ops, SparseCore 0:
  12.7 34.1 reduce-scatter.10
  49.6 31.4 reduce-scatter.14
  83.6 126.1 reduce-scatter.6
  213.4 61.7 reduce-scatter.12
  278.4 60.9 reduce-scatter.16
  343.4 86.9 reduce-scatter.8
  477.5 52.2 all-gather.1
where the time goes:
time: 598 us; the launch traced here: 597 us
  waiting for transfers between devices  394 us (66%)
  blocking collectives  103 us (17%)
  matrix products  38.6 us (6%)
  local copies, waits for them, and re-layouts  35.9 us (6%)
  between operations  16.9 us (3%)
  other arithmetic  8.38 us (1%)
    reduce_scatter x1, waiting for transfers between devices, shards(): lax.psum_scatter(complete[0], 'dp', scatter_dimension=1, tiled=True)  129 us
    reduce_scatter x1, waiting for transfers between devices, shards(): lax.psum_scatter(narrow[0], 'fsdp', scatter_dimension=0, tiled=True)  89.4 us
    reduce_scatter x1, waiting for transfers between devices, shards(): lax.psum_scatter(narrow[1], 'fsdp', scatter_dimension=0, tiled=True)  65.3 us
    reduce_scatter x1, waiting for transfers between devices, shards(): lax.psum_scatter(narrow[2], 'fsdp', scatter_dimension=0, tiled=True)  62.8 us
    psum x1, blocking collectives, shards(): square_sum = lax.psum(local_sum, ('dp', 'fsdp'))  40.3 us
    unnamed x35, local copies, waits for them, and re-layouts  35.9 us
    reduce_scatter x1, waiting for transfers between devices, shards(): lax.psum_scatter(complete[2], 'dp', scatter_dimension=1, tiled=True)  34.1 us
    all_gather x1, blocking collectives, shards(): lax.all_gather(updates[1], 'fsdp', axis=0, tiled=True)  31.6 us
  transfers between devices with their start and end apart: 7, of which 6 were waited for; matrix products, arithmetic and copies ran while one was open for 9% of the time, Pallas kernels for 0%

commit v1 on v0

v1 whole, which is shorter than its diff:
```python
import functools
import math

import jax
import jax.numpy as jnp
from jax import lax
from jax.experimental import pallas as pl
from jax.experimental.pallas import tpu as pltpu
from jax.sharding import PartitionSpec as P

QUERY_OUTPUTS = 8192
KEY_VALUE_OUTS = 1024
PROJECT_RANK = 512
STEP = 10
MESH = pl.DeviceIdType.MESH
CODED = ()
SPAN = 250.0
HALF_SPAN = 125.0
PREFETCH = 3


def log2_of(n):
    return n.bit_length() - 1


def bit_reverse(i, bits):
    out = 0
    for k in range(bits):
        out = out * 2 + (i // (1 << k)) % 2
    return out


def encode(x, inverse):
    level = jnp.abs(x) * inverse
    whole = jnp.floor(level)
    code = jnp.exp2(whole - HALF_SPAN) * (1.0 + (level - whole))
    return jnp.where(x < 0.0, -code, code).astype(jnp.bfloat16)


def decode(code, step):
    y = code.astype(jnp.float32)
    size = jnp.abs(y)
    whole = jnp.floor(jnp.log2(size))
    level = (whole + (HALF_SPAN - 1.0)) + size * jnp.exp2(-whole)
    return jnp.where(y < 0.0, -level, level) * step


class Plan:
    def __init__(self, n_dp, n_fsdp, rank, depth, q_cols, kv_cols):
        self.n_dp, self.n_fsdp = n_dp, n_fsdp
        self.rank, self.depth = rank, depth
        self.q_cols, self.kv_cols = q_cols, kv_cols
        self.width = 2 * kv_cols
        self.n_q = q_cols // self.width
        self.chunks = self.n_q + 1
        self.dp_bits, self.fsdp_bits = log2_of(n_dp), log2_of(n_fsdp)
        self.rows = rank // n_fsdp
        self.half = n_dp // 2
        self.stages = self.dp_bits + self.fsdp_bits

    def order(self, c):
        dp = [("dp", k) for k in range(self.dp_bits)]
        fsdp = [("fsdp", k) for k in range(self.fsdp_bits)]
        if c % 2 == 0:
            return dp + fsdp
        return dp[:1] + fsdp + dp[1:]

    def shapes(self, c):
        out, blocks, rows = [], self.n_dp, self.rank
        for axis, _ in self.order(c):
            if axis == "dp":
                blocks //= 2
            else:
                rows //= 2
            out.append((blocks, rows))
        return out


def reduce_kernel(plan, *refs):
    (gq, gk, gv, ptq, ptk, ptv, avg_q, avg_k, avg_v, sq_q, sq_k, sq_v,
     upd_q, upd_k, upd_v, navg_q, navg_k, navg_v, nsq_q, nsq_k, nsq_v) = refs[:21]
    rest = list(refs[21:])
    (acc, grads, held, sums_dp, sums_fsdp, g_sem, s_sem, r_sem, a_send, a_recv,
     d_send, d_recv, f_send, f_recv, out_sem) = rest[:15]
    rest = rest[15:]
    landing, staging = {}, {}
    for c in range(plan.chunks):
        for s in range(plan.stages):
            landing[c, s] = rest.pop(0)
            if s in CODED:
                staging[c, s] = rest.pop(0)

    n_dp, n_fsdp, width, half = plan.n_dp, plan.n_fsdp, plan.width, plan.half
    me_d, me_f = lax.axis_index("dp"), lax.axis_index("fsdp")

    def bit_of(axis, k):
        return ((me_d if axis == "dp" else me_f) // (1 << k)) % 2

    def partner(axis, k):
        step = (1 - 2 * bit_of(axis, k)) * (1 << k)
        return (me_d + step, me_f) if axis == "dp" else (me_d, me_f + step)

    steps = [(c, j) for c in range(plan.chunks) for j in range(n_dp)]
    core = bit_of("dp", 0)

    def fetches(t):
        c, j = steps[t]
        slot = t % PREFETCH
        low = (1 - core) if j < half else core
        block = low + 2 * bit_reverse(j % half, plan.dp_bits - 1)
        if c < plan.n_q:
            start = pl.multiple_of(block * plan.q_cols + c * width, 128)
            return [pltpu.make_async_copy(
                gq.at[0, :, pl.ds(start, width)], grads.at[slot], g_sem.at[slot, 0])]
        start = pl.multiple_of(block * plan.kv_cols, 128)
        return [
            pltpu.make_async_copy(
                g.at[0, :, pl.ds(start, plan.kv_cols)],
                grads.at[slot, :, pl.ds(at * plan.kv_cols, plan.kv_cols)],
                g_sem.at[slot, at])
            for at, g in enumerate((gk, gv))
        ]

    for t in range(PREFETCH - 1):
        for copy in fetches(t):
            copy.start()

    barrier = pltpu.get_barrier_semaphore()
    for k in range(1, n_dp):
        pl.semaphore_signal(
            barrier, inc=1, device_id=((me_d + k) % n_dp, me_f), device_id_type=MESH)
    for k in range(1, n_fsdp):
        pl.semaphore_signal(
            barrier, inc=1, device_id=(me_d, (me_f + k) % n_fsdp), device_id_type=MESH)
    pl.semaphore_wait(barrier, n_dp + n_fsdp - 2)

    state = {c: (0, n_dp, 0, plan.rank) for c in range(plan.chunks)}
    copies = {}

    def start(c, s):
        axis, k = plan.order(c)[s]
        base_b, blocks, base_r, rows = state[c]
        bit = bit_of(axis, k)
        send_b, send_r = base_b, base_r
        if s == 0:
            blocks //= 2
            send_b, base_b = 0, half
        elif axis == "dp":
            blocks //= 2
            send_b, base_b = base_b + (1 - bit) * blocks, base_b + bit * blocks
        else:
            rows //= 2
            send_r, base_r = base_r + (1 - bit) * rows, base_r + bit * rows
            send_r = pl.multiple_of(send_r, 16)
            base_r = pl.multiple_of(base_r, 16)
        state[c] = (base_b, blocks, base_r, rows)
        if s in CODED:
            src = staging[c, s]
            tile = min(rows, 32)
            for b in range(blocks):
                def largest(i, top, b=b):
                    x = acc[c, send_b + b, pl.ds(pl.multiple_of(send_r + i * tile, 16), tile), :]
                    return jnp.maximum(
                        top, jnp.max(jnp.abs(x).reshape(tile // 8, 8, width), axis=0))
                top = lax.fori_loop(
                    0, rows // tile, largest, jnp.zeros((8, width), jnp.float32))
                top = jnp.max(top, axis=0, keepdims=True)
                top = (jnp.maximum(top, 1e-30) * 1.01).astype(jnp.bfloat16)
                src[b, pl.ds(rows, 16), :] = jnp.broadcast_to(top, (16, width))
                inverse = SPAN / top.astype(jnp.float32)

                def write(i, _, b=b, inverse=inverse):
                    x = acc[c, send_b + b, pl.ds(pl.multiple_of(send_r + i * tile, 16), tile), :]
                    src[b, pl.ds(pl.multiple_of(i * tile, 16), tile), :] = encode(x, inverse)
                    return 0
                lax.fori_loop(0, rows // tile, write, 0)
        else:
            src = acc.at[c, pl.ds(send_b, blocks), pl.ds(send_r, rows), :]
        copy = pltpu.make_async_remote_copy(
            src_ref=src, dst_ref=landing[c, s], send_sem=s_sem.at[c, s],
            recv_sem=r_sem.at[c, s], device_id=partner(axis, k), device_id_type=MESH)
        copy.start()
        copies[c, s] = copy

    def finish(c, s):
        base_b, blocks, base_r, rows = state[c]
        copies[c, s].wait_recv()
        got = landing[c, s]
        tile = min(rows, 32)
        for b in range(blocks):
            if s in CODED:
                step = got[b, pl.ds(rows, 16), :].astype(jnp.float32)[:1] * (1.0 / SPAN)

            def add(i, _, b=b):
                at = pl.ds(pl.multiple_of(base_r + i * tile, 16), tile)
                x = got[b, pl.ds(pl.multiple_of(i * tile, 16), tile), :]
                if s in CODED:
                    x = decode(x, step)
                acc[c, base_b + b, at, :] = acc[c, base_b + b, at, :] + x
                return 0
            lax.fori_loop(0, rows // tile, add, 0)
        if s + 1 < plan.stages:
            start(c, s + 1)

    def multiply(t):
        c, j = steps[t]
        slot = t % PREFETCH
        if t + PREFETCH - 1 < len(steps):
            for copy in fetches(t + PREFETCH - 1):
                copy.start()
        for copy in fetches(t):
            copy.wait()
        if c < plan.n_q:
            tile = min(width, 256)

            def part(i, _):
                at = pl.ds(pl.multiple_of(i * tile, 128), tile)
                acc[c, j, :, at] = jnp.dot(
                    ptq[...], grads[slot, :, at], preferred_element_type=jnp.float32)
                return 0
            lax.fori_loop(0, width // tile, part, 0)
        else:
            for at, pt in enumerate((ptk, ptv)):
                cut = pl.ds(at * plan.kv_cols, plan.kv_cols)
                acc[c, j, :, cut] = jnp.dot(
                    pt[...], grads[slot, :, cut], preferred_element_type=jnp.float32)

    for c in range(plan.chunks):
        for j in range(n_dp):
            multiply(c * n_dp + j)
            if j == half - 1:
                start(c, 0)
        if c > 0:
            finish(c - 1, 0)
    finish(plan.chunks - 1, 0)

    rest_order = [(c, s) for c in range(plan.chunks) for s in range(1, plan.stages)]
    for c, s in sorted(rest_order, key=lambda e: (1.5 * (e[0] // 2) + e[1], e[0])):
        finish(c, s)

    local = jnp.zeros((8, 128), jnp.float32)
    for c in range(plan.chunks):
        base_b, _, base_r, rows = state[c]
        x = acc[c, base_b, pl.ds(base_r, rows), :]
        folded = jnp.sum((x * x).reshape(rows // 8, 8, width), axis=0)
        for i in range(width // 128):
            local = local + folded[:, i * 128:(i + 1) * 128]

    def exchange(value, sums, n, send, recv, peer):
        sums[0] = value
        sent = []
        for k in range(1, n):
            copy = pltpu.make_async_remote_copy(
                src_ref=sums.at[0], dst_ref=sums.at[k], send_sem=send.at[k],
                recv_sem=recv.at[k], device_id=peer(k), device_id_type=MESH)
            copy.start()
            sent.append(copy)
        total = value
        for k, copy in enumerate(sent):
            copy.wait_recv()
            total = total + sums[k + 1]
        return total, sent

    total, sent_d = exchange(
        local, sums_dp, n_dp, d_send, d_recv, lambda k: ((me_d + k) % n_dp, me_f))
    total, sent_f = exchange(
        total, sums_fsdp, n_fsdp, f_send, f_recv, lambda k: (me_d, (me_f + k) % n_fsdp))
    square_sum = jnp.sum(jnp.sum(total, axis=0, keepdims=True), axis=1, keepdims=True)
    threshold = math.sqrt(PROJECT_RANK * (QUERY_OUTPUTS + 2 * KEY_VALUE_OUTS))
    clip = jnp.minimum(1.0, threshold / jnp.sqrt(square_sum + 1e-06))

    rows = plan.rows
    correct_one = 1.0 - 0.9**STEP
    correct_two = 1.0 - 0.95**STEP
    place = pl.multiple_of(bit_reverse(me_f, plan.fsdp_bits) * rows, 16)
    gathers = {}

    def gather_start(c, s):
        k = plan.fsdp_bits - 1 - s
        size = rows << s
        base = pl.multiple_of(bit_reverse(me_f, plan.fsdp_bits) // (1 << s) * size, 16)
        view = held.at[c, pl.ds(base, size), :]
        copy = pltpu.make_async_remote_copy(
            src_ref=view, dst_ref=view, send_sem=a_send.at[c, s], recv_sem=a_recv.at[c, s],
            device_id=partner("fsdp", k), device_id_type=MESH)
        copy.start()
        gathers[c, s] = copy

    def adam(c, cols, avg, sq, navg, nsq, at):
        base_b, _, base_r, _ = state[c]
        scaled = clip * acc[c, base_b, pl.ds(base_r, rows), cols]
        new_avg = 0.9 * avg[:, at] + 0.1 * scaled
        new_sq = 0.95 * sq[:, at] + 0.05 * scaled * scaled
        navg[:, at] = new_avg
        nsq[:, at] = new_sq
        update = new_avg / correct_one / (jnp.sqrt(new_sq / correct_two) + 1e-08)
        held[c, pl.ds(place, rows), cols] = update.astype(jnp.bfloat16)

    kv = plan.kv_cols
    for c in range(plan.chunks):
        if c < plan.n_q:
            adam(c, slice(0, width), avg_q, sq_q, navg_q, nsq_q, slice(c * width, (c + 1) * width))
        else:
            adam(c, slice(0, kv), avg_k, sq_k, navg_k, nsq_k, slice(0, kv))
            adam(c, slice(kv, 2 * kv), avg_v, sq_v, navg_v, nsq_v, slice(0, kv))
        gather_start(c, 0)

    stores = []

    def store(c):
        for f in range(n_fsdp):
            there = pl.ds(bit_reverse(f, plan.fsdp_bits) * rows, rows)
            here = pl.ds(f * rows, rows)
            if c < plan.n_q:
                parts = [(held.at[c, there, :], upd_q.at[here, pl.ds(c * width, width)])]
            else:
                parts = [(held.at[c, there, pl.ds(0, kv)], upd_k.at[here, :]),
                         (held.at[c, there, pl.ds(kv, kv)], upd_v.at[here, :])]
            for src, dst in parts:
                copy = pltpu.make_async_copy(src, dst, out_sem.at[len(stores)])
                copy.start()
                stores.append(copy)

    gather_order = [(c, s) for c in range(plan.chunks) for s in range(plan.fsdp_bits)]
    for c, s in sorted(gather_order, key=lambda e: (e[0] + e[1], e[0])):
        gathers[c, s].wait_recv()
        if s + 1 < plan.fsdp_bits:
            gather_start(c, s + 1)
        else:
            store(c)

    for copy in list(copies.values()) + list(gathers.values()) + sent_d + sent_f:
        copy.wait_send()
    for copy in stores:
        copy.wait()


def apply_kernel(*refs):
    proj, upd, weight, comp, out = (refs[3 * i:3 * i + 3] for i in range(5))
    for p, u, w, c, o in zip(proj, upd, weight, comp, out):
        delta = -0.04 * jnp.dot(p[...], u[...], preferred_element_type=jnp.float32)
        o[...] = w[...].astype(jnp.float32) + (delta + c[...].astype(jnp.float32))


def apply_updates(projectors, updates, weights, comps):
    rows = weights[0].shape[0]
    tile = min(rows, 128)

    def tiled(array):
        return pl.BlockSpec((tile, array.shape[1]), lambda i: (i, 0))

    def whole(array):
        return pl.BlockSpec(array.shape, lambda i: (0, 0))

    args = (*projectors, *updates, *weights, *comps)
    specs = [whole(a) if 3 <= i < 6 else tiled(a) for i, a in enumerate(args)]
    return pl.pallas_call(
        apply_kernel,
        grid=(rows // tile,),
        in_specs=specs,
        out_specs=[tiled(w) for w in weights],
        out_shape=[jax.ShapeDtypeStruct(w.shape, jnp.float32) for w in weights],
        compiler_params=pltpu.CompilerParams(vmem_limit_bytes=40 << 20),
        name="apply_updates",
    )(*args)


def shards(n_dp, n_fsdp, *args):
    gradients, projectors, weights, comps, avgs, squares = (args[3 * i:3 * i + 3] for i in range(6))
    depth, rank = projectors[0].shape
    plan = Plan(n_dp, n_fsdp, rank, depth, weights[0].shape[1], weights[1].shape[1])
    bits = plan.fsdp_bits

    def turned(projector):
        cut = projector.reshape((depth,) + (2,) * bits + (plan.rows,))
        axes = tuple(range(bits, 0, -1)) + (bits + 1, 0)
        return jnp.transpose(cut, axes).reshape(rank, depth)

    scratch = [
        pltpu.VMEM((plan.chunks, n_dp, rank, plan.width), jnp.float32),
        pltpu.VMEM((PREFETCH, depth, plan.width), jnp.bfloat16),
        pltpu.VMEM((plan.chunks, rank, plan.width), jnp.bfloat16),
        pltpu.VMEM((n_dp, 8, 128), jnp.float32),
        pltpu.VMEM((n_fsdp, 8, 128), jnp.float32),
        pltpu.SemaphoreType.DMA((PREFETCH, 2)),
        pltpu.SemaphoreType.DMA((plan.chunks, plan.stages)),
        pltpu.SemaphoreType.DMA((plan.chunks, plan.stages)),
        pltpu.SemaphoreType.DMA((plan.chunks, bits)),
        pltpu.SemaphoreType.DMA((plan.chunks, bits)),
        pltpu.SemaphoreType.DMA((n_dp,)),
        pltpu.SemaphoreType.DMA((n_dp,)),
        pltpu.SemaphoreType.DMA((n_fsdp,)),
        pltpu.SemaphoreType.DMA((n_fsdp,)),
        pltpu.SemaphoreType.DMA(((plan.n_q + 2) * n_fsdp,)),
    ]
    for c in range(plan.chunks):
        for s, (blocks, rows) in enumerate(plan.shapes(c)):
            if s in CODED:
                scratch += [pltpu.VMEM((blocks, rows + 16, plan.width), jnp.bfloat16)] * 2
            else:
                scratch.append(pltpu.VMEM((blocks, rows, plan.width), jnp.float32))

    any_spec = pl.BlockSpec(memory_space=pl.ANY)
    vmem_spec = pl.BlockSpec(memory_space=pltpu.VMEM)
    columns = [w.shape[1] for w in weights]
    moments = [jax.ShapeDtypeStruct(a.shape, jnp.float32) for a in (*avgs, *squares)]
    out = pl.pallas_call(
        functools.partial(reduce_kernel, plan),
        in_specs=[any_spec] * 3 + [vmem_spec] * 9,
        out_specs=[any_spec] * 3 + [vmem_spec] * 6,
        out_shape=[jax.ShapeDtypeStruct((rank, c), jnp.bfloat16) for c in columns] + moments,
        scratch_shapes=scratch,
        compiler_params=pltpu.CompilerParams(
            collective_id=0, has_side_effects=True, vmem_limit_bytes=62 << 20),
        name="project_reduce_gather",
    )(*gradients, *(turned(p) for p in projectors), *avgs, *squares)
    updates, new_avgs, new_sqs = out[:3], out[3:6], out[6:9]
    new_weights = apply_updates(projectors, updates, weights, comps)
    return (*new_weights, *new_avgs, *new_sqs)


def solution(mesh):
    n_dp, n_fsdp = mesh.shape["dp"], mesh.shape["fsdp"]
    grad, proj, cell = P("dp", "fsdp", None), P("fsdp", None), P("fsdp", "dp")
    in_specs = (grad,) * 3 + (proj,) * 3 + (cell,) * 12
    return jax.shard_map(
        functools.partial(shards, n_dp, n_fsdp),
        mesh=mesh, in_specs=in_specs, out_specs=(cell,) * 9, check_vma=False)
```

time: 598 us -> 223 us (0.37)
  waiting for transfers between devices: 394 us -> 0 us
  Pallas kernels: 0 us -> 199 us
  blocking collectives: 103 us -> 0 us
  matrix products: 38.6 us -> 0 us
  between operations: 16.9 us -> 0.75 us
  local copies, waits for them, and re-layouts: 35.9 us -> 21.3 us
  other arithmetic: 8.38 us -> 0 us
    reduce_scatter x6 -> x0, waiting for transfers between devices: 394 us -> none  [the longest x1 129 us: shards(): lax.psum_scatter(complete[0], 'dp', scatter_dimension=1, tiled=True)]
    pallas_call x0 -> x2, Pallas kernels: none -> 199 us  [the longest x1 190 us: shards(): pl.pallas_call(functools.partial(reduce_kernel, plan), in_specs=[any_spec...]
    all_gather x2 -> x0, blocking collectives: 62.5 us -> none  [the longest x1 31.6 us: shards(): lax.all_gather(updates[1], 'fsdp', axis=0, tiled=True)]
    psum x1 -> x0, blocking collectives: 40.3 us -> none  [shards(): square_sum = lax.psum(local_sum, ('dp', 'fsdp'))]
    dot_general x6 -> x0, matrix products: 38.6 us -> none  [the longest x3 23.9 us: shards(): lax.dot_general(projector, gradient, contract_rows, preferred_element_typ...]
    unnamed x35 -> x47, local copies, waits for them, and re-layouts: 35.9 us -> 18.1 us
  transfers between devices with their start and end apart: 7 -> 0, of which waited for: 6 -> 0; matrix products, arithmetic and copies ran while one was open for 9% -> 0% of each run, Pallas kernels for 0% -> 0%
where the time goes in v1:
time: 223 us; the launch traced here: 221 us
  Pallas kernels  199 us (89%)
  local copies, waits for them, and re-layouts  21.3 us (10%)
    pallas_call x1, Pallas kernels, shards(): pl.pallas_call(functools.partial(reduce_kernel, plan), in_specs=[any_spec...  190 us
    unnamed x47, local copies, waits for them, and re-layouts  18.1 us
    pallas_call x1, Pallas kernels, apply_updates(): pl.pallas_call(apply_kernel, grid=(rows // tile,), in_specs=specs, out_sp...  9.48 us

profile of v1, /device:TPU:0, one launch (start us, length us, event | category | flops | bytes accessed | tf_op | source)
XLA Modules:
  0.0 221.2 jit_solution(12838598888701687806)
XLA Ops:
  0.6 0.0 copy-start.3
  0.7 1.6 copy.30
  2.3 1.1 copy.31
  3.4 0.5 copy.32
  3.9 1.1 copy.33
  5.0 0.5 copy.34
  5.5 1.1 copy.35
  6.6 189.6 %project_reduce_gather.1 = (bf16[512,2048]{1,0:T(8,128)(2,1)}, bf16[512,256]{1,0:T(8,128)(2,1)}, bf16[512,256]{1,0:T(8,128)(2,1)}, f32[64,2048]{1,0:T(8,128)}, f...) custom-call(bf16[1,1024,8192]{2,1,0:T(8,128)(2,1)} %refs_0_.2, ...), custom_call_target="tpu_custom_call" | custom-call | tf_op jit(solution)/shard_map/project_reduce_gather/pallas_call | solution.py:407
  196.3 1.2 copy-done.2
  197.5 1.2 copy-done.4
  198.7 2.2 copy-done.5
  200.9 1.6 copy-done.6
  202.5 1.0 copy-done.8
  203.5 1.0 copy-done.9
  204.6 1.0 copy-done.10
  205.6 0.9 copy-done.11
  206.6 0.9 copy-done.12
  207.6 9.5 %apply_updates.1 = (f32[1024,2048]{1,0:T(8,128)}, f32[1024,256]{1,0:T(8,128)}, f32[1024,256]{1,0:T(8,128)}) custom-call(bf16[1024,512]{1,0:T(8,128)(2,1)S(1)} %copy-done, bf16[1024,512]{1,0:T(8,128)(2,1)S(1)} %copy-done.2, bf16[1024,512]{1,0:T(8,128)(2,1)S(1)} %copy-done.4, bf16[512,2048]{1,0:T(8,128)(2,1)S(1)} %copy-done.6, ...), custom_call_target="tpu_custom_call" | custom-call | tf_op jit(solution)/shard_map/apply_updates/pallas_call | solution.py:357
  217.0 0.8 copy.42
  217.8 0.6 copy.43
  218.5 0.6 copy.44
  219.1 0.8 copy.45
  219.9 0.6 copy.46
  220.5 0.6 copy.47
  (28 shorter events, 0.1 us)
Async XLA Ops:
  0.6 4.4 %copy-start.3 = (bf16[1024,512]{1,0:T(8,128)(2,1)S(1)}, bf16[1024,512]{1,0:T(8,128)(2,1)}, u32[]{:S(2)}) copy-start(bf16[1024,512]{1,0:T(8,128)(2,1)} %refs_2_.3) | copy-start | bytes 3145732
  0.7 2.7 %copy-start.1 = (bf16[1024,512]{1,0:T(8,128)(2,1)S(1)}, bf16[1024,512]{1,0:T(8,128)(2,1)}, u32[]{:S(2)}) copy-start(bf16[1024,512]{1,0:T(8,128)(2,1)} %refs_1_.3) | copy-start | bytes 3145732
  6.6 189.6 %copy-start = (bf16[1024,512]{1,0:T(8,128)(2,1)S(1)}, bf16[1024,512]{1,0:T(8,128)(2,1)}, u32[]{:S(2)}) copy-start(bf16[1024,512]{1,0:T(8,128)(2,1)} %refs_0_.3) | copy-start | bytes 3145732
  6.6 189.6 %copy-start.7 = (bf16[1024,256]{1,0:T(8,128)(2,1)S(1)}, bf16[1024,256]{1,0:T(8,128)(2,1)}, u32[]{:S(2)}) copy-start(bf16[1024,256]{1,0:T(8,128)(2,1)} %refs_7_.3) | copy-start | bytes 1572868
  196.3 1.2 copy-start.2
  197.5 1.2 copy-start.4
  198.7 2.2 copy-start.5
  200.9 1.6 copy-start.6
  202.5 1.0 copy-start.8
  203.5 1.0 copy-start.9
  204.6 1.0 copy-start.10
  205.6 0.9 copy-start.11
  206.6 0.9 copy-start.12
  207.5 9.5 %copy-start.14 = (f32[64,2048]{1,0:T(8,128)S(1)}, f32[64,2048]{1,0:T(8,128)}, u32[]{:S(2)}) copy-start(f32[64,2048]{1,0:T(8,128)} %get-tuple-element.45) | copy-start | bytes 1572868
  207.5 10.3 %copy-start.18 = (f32[64,256]{1,0:T(8,128)S(1)}, f32[64,256]{1,0:T(8,128)}, u32[]{:S(2)}) copy-start(f32[64,256]{1,0:T(8,128)} %get-tuple-element.46) | copy-start | bytes 196612
  207.5 10.9 %copy-start.17 = (f32[64,256]{1,0:T(8,128)S(1)}, f32[64,256]{1,0:T(8,128)}, u32[]{:S(2)}) copy-start(f32[64,256]{1,0:T(8,128)} %get-tuple-element.47) | copy-start | bytes 196612
  207.5 11.6 %copy-start.13 = (f32[64,2048]{1,0:T(8,128)S(1)}, f32[64,2048]{1,0:T(8,128)}, u32[]{:S(2)}) copy-start(f32[64,2048]{1,0:T(8,128)} %get-tuple-element.48) | copy-start | bytes 1572868
  207.5 12.4 %copy-start.16 = (f32[64,256]{1,0:T(8,128)S(1)}, f32[64,256]{1,0:T(8,128)}, u32[]{:S(2)}) copy-start(f32[64,256]{1,0:T(8,128)} %get-tuple-element.49) | copy-start | bytes 196612
  207.5 13.0 %copy-start.15 = (f32[64,256]{1,0:T(8,128)S(1)}, f32[64,256]{1,0:T(8,128)}, u32[]{:S(2)}) copy-start(f32[64,256]{1,0:T(8,128)} %get-tuple-element.50) | copy-start | bytes 196612
